TPU v7x, 128 devices: a whole 4x4x4 slice. The times are simulated.
128 devices in a mesh: surf: 32 (over x, y, core), dir: 4 (over z).
Axes of the slice: x: 4, y: 4, z: 4, core: 2. Of those that a mesh axis runs over, the one named last changes fastest.
Arguments:
- densities: float32 [512, 32768], P(None, ('surf', 'dir')), may hold values from -6 to 6
- weights: float32 [32768], P(('surf', 'dir')), may hold values from 0.1 to 1
- coords: float32 [3, 32768], P(None, ('surf', 'dir')), may hold values from -1 to 1
- counts: int32 [128], P(('surf', 'dir')), may hold values from 0 to 256, as said below
- wave: float32 [3, 4, 8192], P(None, 'dir'), may hold values from -20 to 20
Outputs:
- pattern: float32 [512, 4, 8192], P(None, 'dir', 'surf')
Inputs may be any that keep to these rules, and one draw needn't show every extreme that they name: The counts sum to 16384. For every device q, the counts of the devices before q sum to between q * 128 and (q + 1) * 128. One count equals 256 and one equals 0.
All inputs are finite; a program needn't handle non-finite values.
Results may differ from a plain program's by a relative error of at most 0.0037.
Values sent between devices are 32-bit elements; how exact they have to be, the bound alone decides.
A program may use at most 128 MiB of HBM per device.

v0:
```python
import math

import jax
import jax.numpy as jnp
from jax import lax
from jax.sharding import PartitionSpec as P

PB_DEV = 128


def block_terms(strength, xyz, kvec):
    phase = (
        xyz[0][:, None] * kvec[0][None, :]
        + xyz[1][:, None] * kvec[1][None, :]
        + xyz[2][:, None] * kvec[2][None, :]
    )
    cosine = lax.optimization_barrier(jnp.cos(phase).astype(jnp.bfloat16)).astype(jnp.float32)
    sine = lax.optimization_barrier(jnp.sin(phase).astype(jnp.bfloat16)).astype(jnp.float32)
    first = jnp.dot(strength, cosine, precision=lax.Precision.HIGHEST)
    second = jnp.dot(strength, sine, precision=lax.Precision.HIGHEST)
    half = strength.shape[0] // 2
    return jnp.concatenate([first[:half] + second[half:], first[half:] - second[:half]], axis=0)


def local(densities, weights, coords, counts, wave):
    slots = weights.shape[0]
    processor_roster = lax.axis_size(("surf", "dir"))
    scale_factor = 1.0 / math.sqrt(PB_DEV * processor_roster)
    slot_ids = jnp.arange(slots, dtype=jnp.int32)
    scaled = weights[None, :] * densities * scale_factor
    rounded = lax.optimization_barrier(
        jnp.where((slot_ids < counts[0])[None, :], scaled, 0.0).astype(jnp.bfloat16)
    )
    plane_harmonic = rounded.astype(jnp.float32)
    kvec = wave[:, 0, :]
    total = block_terms(
        lax.all_gather(plane_harmonic, "dir", axis=1, tiled=True),
        lax.all_gather(coords, "dir", axis=1, tiled=True),
        kvec,
    )
    share = lax.psum_scatter(total, "surf", scatter_dimension=1, tiled=True)
    return share[:, None, :]


def solution(mesh):
    placed = (
        P(None, ("surf", "dir")),
        P(("surf", "dir")),
        P(None, ("surf", "dir")),
        P(("surf", "dir")),
        P(None, "dir", None),
    )
    return jax.shard_map(
        local, mesh=mesh, in_specs=placed, out_specs=P(None, "dir", "surf"), check_vma=False
    )
```

profile of v0, /device:TPU:1, one launch (start us, length us, event | category | flops | bytes accessed | tf_op | source)
XLA Modules:
  0.0 364.1 jit_solution(156126383973113246)
XLA Ops:
  6.5 0.0 all-gather.2.cloned.1.call-start
  7.2 1.1 select_convert_fusion
  8.3 0.8 convert_element_type.15
  9.1 0.0 all-gather.2.cloned.1.call-update
  9.2 0.0 reduce-scatter.2.cloned.1.call-start
  9.2 0.8 fusion
  10.0 11.2 %all_gather.7 = f32[3,1024]{1,0:T(4,128)S(1)} all-gather(f32[3,256]{1,0:T(4,128)} %param.7), channel_id=1, replica_groups=mesh['surf'=32,'dir'=4] {'dir'}, dimensions={1}, use_global_device_ids=true | all-gather | bytes 15360 | tf_op jit(solution)/shard_map/all_gather | solution.py:38
  21.2 125.3 %cosine_convert_fusion = (bf16[1024,8192]{1,0:T(8,128)(2,1)}, bf16[1024,8192]{1,0:T(8,128)(2,1)}) fusion(f32[8192]{0:T(1024)S(1)} %bitcast.15, f32[1024]{0:T(1024)S(1)} %bitcast.18, f32[8192]{0:T(1024)S(1)} %bitcast.16, f32[1024]{0:T(1024)S(1)} %bitcast.19, f32[8192]{0:T(1024)S(1)} %bitcast.14, f32[1024]{0:T(1024)S(1)} %bitcast.17), kind=kLoop, calls=%fused_computation.1 | loop fusion | flops 58720256 | bytes 33665024 | tf_op jit(solution)/shard_map/convert_element_type | solution.py:17
  146.6 0.0 all-gather.2.cloned.1.call-done
  146.6 0.0 copy-start
  146.6 0.0 copy-start.1
  146.6 31.9 %fusion.2 = f32[512,8192]{1,0:T(8,128)} fusion(f32[512,1024]{1,0:T(8,128)} %all-gather.2.cloned.1.call-done, bf16[1024,8192]{1,0:T(8,128)(2,1)} %get-tuple-element.7), kind=kOutput, calls=%fused_computation.10 | convolution fusion | flops 51539607552 | bytes 35651584 | tf_op jit(solution)/shard_map/dot_general | solution.py:19
  178.5 0.0 copy-done
  178.5 0.0 copy-done.1
  178.5 28.9 %fusion.3 = f32[512,8192]{1,0:T(8,128)} fusion(f32[512,1024]{1,0:T(8,128)S(1)} %copy-done.1, bf16[1024,8192]{1,0:T(8,128)(2,1)S(1)} %copy-done), kind=kOutput, calls=%fused_computation.11 | convolution fusion | flops 51539607552 | bytes 35651584 | tf_op jit(solution)/shard_map/dot_general | solution.py:20
  207.3 18.0 %slice_add_fusion = (f32[256,8192]{1,0:T(8,128)}, f32[256,8192]{1,0:T(8,128)}) fusion(f32[512,8192]{1,0:T(8,128)} %fusion.3, f32[512,8192]{1,0:T(8,128)} %fusion.2), kind=kLoop, calls=%fused_computation.5 | loop fusion | flops 4194304 | bytes 50331648 | tf_op jit(solution)/shard_map/add | solution.py:22
  225.3 11.6 %pad_maximum_fusion = f32[512,8192]{1,0:T(8,128)} fusion(f32[256,8192]{1,0:T(8,128)} %get-tuple-element.6, f32[256,8192]{1,0:T(8,128)} %get-tuple-element.5), kind=kLoop, calls=%fused_computation.3 | loop fusion | flops 4194304 | bytes 33554432 | tf_op jit(solution)/shard_map/concatenate | solution.py:22
  237.0 0.0 reduce-scatter.2.cloned.1.call-update
  237.0 117.9 %reduce-scatter.2.cloned.1.call-done = f32[512,256]{1,0:T(8,128)} async-done(((f32[512,8192]{1,0:T(8,128)}), f32[512,256]{1,0:T(8,128)}) %reduce-scatter.2.cloned.1.call-update) | async-done | bytes 524304 | tf_op jit(solution)/shard_map/reduce_scatter | solution.py:41
  354.9 2.4 copy.6
  (2 shorter events, 0.0 us)
Async XLA Ops:
  6.5 140.1 %all-gather.2.cloned.1.call-start = ((), (), s32[]{:S(2)}) async-start(), calls=%async_computation.1 | async-start | bytes 2621440 | tf_op jit(solution)/shard_map/all_gather | solution.py:37
  9.2 345.7 %reduce-scatter.2.cloned.1.call-start = ((), (), s32[]{:S(2)}) async-start(), calls=%async_computation.2 | async-start | bytes 17301504 | tf_op jit(solution)/shard_map/reduce_scatter | solution.py:41
  146.6 31.9 %copy-start = (bf16[1024,8192]{1,0:T(8,128)(2,1)S(1)}, bf16[1024,8192]{1,0:T(8,128)(2,1)}, u32[]{:S(2)}) copy-start(bf16[1024,8192]{1,0:T(8,128)(2,1)} %get-tuple-element.8) | copy-start | bytes 50331652
  146.6 31.9 %copy-start.1 = (f32[512,1024]{1,0:T(8,128)S(1)}, f32[512,1024]{1,0:T(8,128)}, u32[]{:S(2)}) copy-start(f32[512,1024]{1,0:T(8,128)} %all-gather.2.cloned.1.call-done) | copy-start | bytes 6291460
Sparse Core Ops, SparseCore 0:
  9.3 34.2 all-gather.1
  237.1 117.7 reduce-scatter.1
where the time goes:
time: 365 us; the launch traced here: 364 us
  other arithmetic  157 us (43%)
  waiting for transfers between devices  118 us (32%)
  matrix products  60.7 us (17%)
  between operations  14.1 us (4%)
  blocking collectives  11.2 us (3%)
    convert_element_type x1, other arithmetic, block_terms(): jnp.cos(phase).astype(jnp.bfloat16)  125 us
    reduce_scatter x1, waiting for transfers between devices, local(): share = lax.psum_scatter(total, 'surf', scatter_dimension=1, tiled=True)  118 us
    dot_general x1, matrix products, block_terms(): first = jnp.dot(strength, cosine, precision=lax.Precision.HIGHEST)  31.9 us
    dot_general x1, matrix products, block_terms(): second = jnp.dot(strength, sine, precision=lax.Precision.HIGHEST)  28.9 us
    add x1, other arithmetic, block_terms(): first[:half] + second[half:]  18 us
    concatenate x1, other arithmetic, block_terms(): jnp.concatenate([first[:half] + second[half:], first[half:] - second[:hal...  11.6 us
    all_gather x1, blocking collectives, local(): lax.all_gather(coords, 'dir', axis=1, tiled=True)  11.2 us
  transfers between devices with their start and end apart: 2, of which 1 were waited for; matrix products, arithmetic and copies ran while one was open for 35% of the time, Pallas kernels for 0%

commit v1 on v0

v1 whole, which is shorter than its diff:
```python
import functools
import math

import numpy as np

import jax
import jax.numpy as jnp
from jax import lax
from jax.experimental import pallas as pl
from jax.experimental.pallas import tpu as pltpu
from jax.sharding import PartitionSpec as P

MESH = pl.DeviceIdType.MESH
F32, BF16, I32 = jnp.float32, jnp.bfloat16, jnp.int32
N = 4
PTS = 128
NCH = 4
HB = 64
NDIR = 2048
BLK = 256


def _fit(f, terms, odd):
    x = np.cos(np.linspace(0, np.pi / 2, 2001)) * 0.5
    a = np.stack([x ** (2 * k + odd) for k in range(terms)], 1)
    w = np.ones_like(x)
    for _ in range(60):
        c = np.linalg.lstsq(a * w[:, None], f(x) * w, rcond=None)[0]
        e = np.abs(a @ c - f(x))
        w = w * np.sqrt(e / e.max() + 0.02)
        w = w / w.max()
    return [float(np.float32(v)) for v in c * math.sqrt(2.0)]


SIN = _fit(lambda r: np.sin(np.pi * r), 3, 1)
COS = _fit(lambda r: np.cos(np.pi * r), 4, 0)


def horner(q, c):
    acc = c[-1] * q + c[-2]
    for k in c[-3::-1]:
        acc = acc * q + k
    return acc


def split3(v):
    a = v.astype(BF16).astype(F32)
    b = (v - a).astype(BF16).astype(F32)
    return a, b, (v - a) - b


E_STEPS = {
    0: [(1, 0)], 1: [(0, 1)], 2: [(2, 0)], 3: [(0, 2)], 4: [(1, 1)], 5: [(3, 0)], 6: [(1, 2)], 7: [(0, 3)],
    8: [(2, 1)], 9: [(2, 2)], 10: [(1, 3)], 11: [(3, 1)], 12: [(0, 4)], 13: [(3, 2)], 14: [(2, 3)], 15: [],
}
M_STEPS = {1: [(1, 4)], 2: [(3, 3)], 6: [(2, 4)], 10: [(3, 4)]}


def kernel(
    dens, wts, coords, counts, wave, out,
    cnt1, cnt2, crd, cin, cout, kf, kmat, keep, sout, sin_, G, E, L, Pm, Po, Cx, Hp, Hm, Rp, Rm,
    s1s, s1r, s2s, s2r, scs, scr, sgs, sgr, shs, shr, ggs, ggr, cxs, cxr, hs, hr, rs, rr,
):
    surf, z = lax.axis_index("surf"), lax.axis_index("dir")
    x, y, c = surf // 8, (surf // 2) % N, surf % 2
    q = surf * N + z

    def dev(xx, yy, cc, zz):
        return ((xx * N + yy) * 2 + cc, zz)

    def up(v, k):
        return lax.rem(v + (k + N), N)

    def remote(src, dst, ss, rs_, to):
        return pltpu.make_async_remote_copy(
            src_ref=src, dst_ref=dst, send_sem=ss, recv_sem=rs_, device_id=to, device_id_type=MESH
        )

    me8 = c * N + z
    peers8 = []
    for k in range(1, 8):
        o = lax.rem(me8 + k, 8)
        peers8.append(dev(x, y, o // N, lax.rem(o, N)))
    peers16 = [dev(up(x, i), up(y, j), c, z) for i in range(N) for j in range(N) if i or j]
    peersyz = [(i, j) for i in range(N) for j in range(N) if i or j]
    qn, qp = lax.rem(q + 1, 128), lax.rem(q + 127, 128)
    nxt, prv = (qn // N, lax.rem(qn, N)), (qp // N, lax.rem(qp, N))

    barrier = pltpu.get_barrier_semaphore()
    extra = [dev(x, up(y, i), c, up(z, j)) for i, j in peersyz if i and j]
    greet = peers8 + peers16 + extra + [nxt, prv]
    for to in greet:
        pl.semaphore_signal(barrier, inc=1, device_id=to, device_id_type=MESH)

    kf[...] = jnp.zeros_like(kf)
    for t, dx in enumerate((2, 1, 3, 0)):
        for h in range(2):
            cc = c if h == 0 else 1 - c
            at = pl.multiple_of((up(x, dx) * 8 + y * 2 + cc) * BLK, BLK)
            for k in range(3):
                kf[k : k + 1, t * 512 + h * BLK : t * 512 + (h + 1) * BLK] = (
                    wave[k, :, pl.ds(at, BLK)] * (1.0 / (2.0 * math.pi))
                )
    k1, k2, k3 = split3(kf[...])
    kmat[...] = jnp.concatenate([k1, k2, k1, k3, k2, k1, jnp.zeros((80, NDIR), F32)], 0).astype(BF16)
    cin[...] = jnp.zeros_like(cin)
    cin[0:3, :] = coords[...]
    cnt = counts[0]
    cnt1[me8] = jnp.full((8, 128), cnt, I32)

    pl.semaphore_wait(barrier, len(greet))

    n1 = [
        remote(cnt1.at[me8], cnt1.at[me8], s1s.at[k], s1r.at[k], peers8[k]) for k in range(7)
    ]
    for d in n1:
        d.start()
    for d in n1:
        d.wait_recv()
    total8 = jnp.zeros((8, 128), I32)
    before = jnp.zeros((8, 128), I32)
    for k in range(8):
        v = cnt1[k]
        total8 = total8 + v
        before = before + v * jnp.where(k < me8, 1, 0)
    me16 = x * N + y
    cnt2[me16] = total8
    n2 = [
        remote(cnt2.at[me16], cnt2.at[me16], s2s.at[k], s2r.at[k], peers16[k]) for k in range(15)
    ]
    for d in n2:
        d.start()
    for d in n2:
        d.wait_recv()
    for k in range(16):
        before = before + cnt2[k] * jnp.where(k < me16, 1, 0)
    shift = before - q * PTS

    srow = jnp.broadcast_to(shift[0:1, :], (256, 128))
    srow = jnp.concatenate([srow, srow], 1)
    slot = lax.broadcasted_iota(I32, (256, 256), 0)
    col = lax.broadcasted_iota(I32, (256, 256), 1)
    pick = jnp.where((col - slot == srow) & (slot < cnt), 1.0, 0.0).astype(BF16)

    ca, cb, cc_ = split3(cin[...])
    cp = jnp.dot(jnp.concatenate([ca, cb, cc_], 0).astype(BF16), pick, preferred_element_type=F32)
    packed = cp[0:8] + cp[8:16] + cp[16:24]
    cout[...] = packed[:, 128:]
    dc = remote(cout, crd.at[16], scs.at[0], scr.at[0], nxt)
    dc.start()

    scale = 1.0 / math.sqrt(PTS * 128)
    w = wts[...]
    dsh = []
    for ch in range(NCH):
        ra, rb = slice(ch * HB, (ch + 1) * HB), slice(256 + ch * HB, 256 + (ch + 1) * HB)
        v = jnp.concatenate([dens[ra, :], dens[rb, :]], 0)
        v = ((w * v) * scale).astype(BF16)
        moved = jnp.dot(v, pick, preferred_element_type=F32)
        keep[ch] = moved[:, :128]
        sout[ch] = moved[:, 128:]
        d = remote(sout.at[ch], sin_.at[ch], shs.at[ch], shr.at[ch], nxt)
        d.start()
        dsh.append(d)

    own = y * N + z
    dc.wait_recv()
    crd[own] = packed[:, :128] + crd[16]
    dg = [
        remote(crd.at[own], crd.at[own], sgs.at[k], sgr.at[k], dev(x, up(y, i), c, up(z, j)))
        for k, (i, j) in enumerate(peersyz)
    ]
    for d in dg:
        d.start()

    def gcopies(ch, st):
        sem = lambda n: (ggs.at[ch, st * 4 + n], ggr.at[ch, st * 4 + n])
        yn, yp, zn, zp = (dev(x, up(y, 1), c, z), dev(x, up(y, -1), c, z), dev(x, y, c, up(z, 1)), dev(x, y, c, up(z, -1)))
        ym, yq, zm, zq = up(y, -1), up(y, 1), up(z, -1), up(z, 1)
        lo, lo1, lo2 = pl.ds(0, 64), pl.ds(0, 32), pl.ds(32, 32)
        hi, hi1, hi2 = pl.ds(64, 64), pl.ds(64, 32), pl.ds(96, 32)
        al = pl.ds(0, N)
        if st == 0:
            parts = [((y, z, lo), yn), ((y, z, lo), yp), ((y, z, hi), zn), ((y, z, hi), zp)]
        elif st == 1:
            parts = [((ym, z, lo1), yn), ((yq, z, lo2), yp), ((y, zm, hi1), zn), ((y, zq, hi2), zp)]
        elif st == 2:
            parts = [((al, z, lo), zn), ((al, z, lo), zp), ((y, al, hi), yn), ((y, al, hi), yp)]
        else:
            parts = [((al, zm, lo1), zn), ((al, zq, lo2), zp), ((ym, al, hi1), yn), ((yq, al, hi2), yp)]
        return [remote(G.at[(ch,) + p], G.at[(ch,) + p], *sem(n), to) for n, (p, to) in enumerate(parts)]

    def gstep(ch, st):
        if st == 0:
            dsh[ch].wait_recv()
            G[ch, y, z] = keep[ch] + sin_[ch]
        else:
            for d in gcopies(ch, st - 1):
                d.wait_recv()
        if st < 4:
            for d in gcopies(ch, st):
                d.start()

    gstep(0, 0)

    @pl.loop(0, 16)
    def _(it):
        @pl.when(it == 1)
        def _():
            for d in dg:
                d.wait_recv()

        b = lax.rem(own + it, 16)
        a1, a2, a3 = split3(crd[b])
        xt = jnp.concatenate([a1, a1, a2, a1, a2, a3, jnp.zeros((80, 128), F32)], 0)
        xm = xt.T.astype(BF16)
        rows = pl.multiple_of(b * PTS, PTS)
        for j in range(NDIR // 256):
            cols = slice(j * 256, (j + 1) * 256)
            turn = jnp.dot(xm, kmat[:, cols], preferred_element_type=F32)
            r = turn - jnp.round(turn)
            r2 = r * r
            s = r * horner(r2, SIN)
            E[pl.ds(rows, PTS), cols] = (1.0 - s * s).astype(BF16)
            E[pl.ds(pl.multiple_of(rows + 2048, PTS), PTS), cols] = (s * horner(r2, COS)).astype(BF16)
        for i, steps in E_STEPS.items():
            if steps:
                @pl.when(it == i)
                def _():
                    for ch, st in steps:
                        gstep(ch, st)

    xn, xp, other = dev(up(x, 1), y, c, z), dev(up(x, -1), y, c, z), dev(x, y, 1 - c, z)

    def core_copy(m):
        return remote(Po.at[m], Cx.at[m], cxs.at[m], cxr.at[m], other)

    def half_copy(ch, n):
        land, to = ((Hp, xn), (Hm, xp))[n]
        k = n * NCH + ch
        return remote(Pm.at[ch * 4, pl.ds(64 * n, 64)], land.at[ch], hs.at[k], hr.at[k], to)

    def full_copy(ch, n):
        land, to = ((Rp, xn), (Rm, xp))[n]
        k = n * NCH + ch
        return remote(Pm.at[ch * 4 + 1 + n], land.at[ch], rs.at[k], rr.at[k], to)

    def after_core(m):
        core_copy(m).wait_recv()
        Pm[m] = Pm[m] + Cx[m]
        ch, t = m // 4, lax.rem(m, 4)

        @pl.when(t == 0)
        def _():
            half_copy(ch, 0).start()
            half_copy(ch, 1).start()

        @pl.when(t == 1)
        def _():
            half_copy(ch, 0).wait_recv()
            Pm[m, 0:64] = Pm[m, 0:64] + Hp[ch]
            full_copy(ch, 0).start()

        @pl.when(t == 2)
        def _():
            half_copy(ch, 1).wait_recv()
            Pm[m, 64:128] = Pm[m, 64:128] + Hm[ch]
            full_copy(ch, 1).start()

    def finish(ch):
        full_copy(ch, 0).wait_recv()
        full_copy(ch, 1).wait_recv()
        res = Pm[ch * 4 + 3] + Rp[ch] + Rm[ch]
        out[pl.ds(pl.multiple_of(ch * HB, HB), HB), :] = res[0:64]
        out[pl.ds(pl.multiple_of(256 + ch * HB, HB), HB), :] = res[64:128]

    @pl.loop(0, 4 * NCH)
    def _(m):
        ch, t = m // 4, lax.rem(m, 4)

        @pl.when(t == 0)
        def _():
            for b in range(16):
                g = G[ch, b // N, b % N]
                lo, hi = g[0:64].astype(BF16), g[64:128].astype(BF16)
                cols, cols2 = slice(b * PTS, (b + 1) * PTS), slice(2048 + b * PTS, 2048 + (b + 1) * PTS)
                L[0:64, cols] = lo
                L[0:64, cols2] = hi
                L[64:128, cols] = hi
                L[64:128, cols2] = -lo

        part = jnp.dot(L[...], E[:, pl.ds(pl.multiple_of(t * 512, 512), 512)], preferred_element_type=F32)
        Pm[m] = part[:, :BLK]
        Po[m] = part[:, BLK:]
        core_copy(m).start()
        for i, steps in M_STEPS.items():
            @pl.when(m == i)
            def _():
                for ch_, st in steps:
                    gstep(ch_, st)

        @pl.when(m > 0)
        def _():
            after_core(m - 1)

        @pl.when((t == 2) & (m > 4))
        def _():
            finish(ch - 1)

    after_core(4 * NCH - 1)
    finish(NCH - 1)

    for d in n1 + n2 + [dc] + dsh + dg:
        d.wait_send()
    for ch in range(NCH):
        for st in range(4):
            for d in gcopies(ch, st):
                d.wait_send()
        for n in range(2):
            half_copy(ch, n).wait_send()
            full_copy(ch, n).wait_send()
        for t in range(4):
            core_copy(ch * 4 + t).wait_send()


def local(densities, weights, coords, counts, wave):
    vm = pl.BlockSpec(memory_space=pltpu.VMEM)
    dma = pltpu.SemaphoreType.DMA
    out = pl.pallas_call(
        kernel,
        out_shape=jax.ShapeDtypeStruct((512, BLK), F32),
        in_specs=[vm, vm, vm, pl.BlockSpec(memory_space=pltpu.SMEM), vm],
        out_specs=vm,
        scratch_shapes=[
            pltpu.VMEM((8, 8, 128), I32),
            pltpu.VMEM((16, 8, 128), I32),
            pltpu.VMEM((17, 8, 128), F32),
            pltpu.VMEM((8, 256), F32),
            pltpu.VMEM((8, 128), F32),
            pltpu.VMEM((8, NDIR), F32),
            pltpu.VMEM((128, NDIR), BF16),
            pltpu.VMEM((NCH, 128, 128), F32),
            pltpu.VMEM((NCH, 128, 128), F32),
            pltpu.VMEM((NCH, 128, 128), F32),
            pltpu.VMEM((NCH, N, N, 128, 128), F32),
            pltpu.VMEM((4096, NDIR), BF16),
            pltpu.VMEM((128, 4096), BF16),
            pltpu.VMEM((16, 128, BLK), F32),
            pltpu.VMEM((16, 128, BLK), F32),
            pltpu.VMEM((16, 128, BLK), F32),
            pltpu.VMEM((NCH, 64, BLK), F32),
            pltpu.VMEM((NCH, 64, BLK), F32),
            pltpu.VMEM((NCH, 128, BLK), F32),
            pltpu.VMEM((NCH, 128, BLK), F32),
            dma((7,)), dma((7,)),
            dma((15,)), dma((15,)),
            dma((1,)), dma((1,)),
            dma((15,)), dma((15,)),
            dma((NCH,)), dma((NCH,)),
            dma((NCH, 16)), dma((NCH, 16)),
            dma((16,)), dma((16,)),
            dma((2 * NCH,)), dma((2 * NCH,)),
            dma((2 * NCH,)), dma((2 * NCH,)),
        ],
        compiler_params=pltpu.CompilerParams(
            collective_id=0, has_side_effects=True, vmem_limit_bytes=56 * 2**20
        ),
        cost_estimate=pl.CostEstimate(flops=8_600_000_000, bytes_accessed=2_000_000, transcendentals=0),
        name="far_field",
    )(densities, weights.reshape(1, -1), coords, counts, wave)
    return out[:, None, :]


def solution(mesh):
    placed = (
        P(None, ("surf", "dir")),
        P(("surf", "dir")),
        P(None, ("surf", "dir")),
        P(("surf", "dir")),
        P(None, "dir", None),
    )
    return jax.shard_map(
        local, mesh=mesh, in_specs=placed, out_specs=P(None, "dir", "surf"), check_vma=False
    )
```

time: 365 us -> 90.2 us (0.25)
  other arithmetic: 157 us -> 0 us
  waiting for transfers between devices: 118 us -> 0 us
  Pallas kernels: 0 us -> 87 us
  matrix products: 60.7 us -> 0 us
  between operations: 14.1 us -> 0.66 us
  blocking collectives: 11.2 us -> 0 us
    convert_element_type x3 -> x0, other arithmetic: 127 us -> none  [the longest x1 125 us: block_terms(): jnp.cos(phase).astype(jnp.bfloat16)]
    reduce_scatter x1 -> x0, waiting for transfers between devices: 118 us -> none  [local(): share = lax.psum_scatter(total, 'surf', scatter_dimension=1, tiled=True)]
    pallas_call x0 -> x1, Pallas kernels: none -> 87 us  [local(): pl.pallas_call(kernel, out_shape=jax.ShapeDtypeStruct((512, BLK), F32), i...]
    dot_general x2 -> x0, matrix products: 60.7 us -> none  [the longest x1 31.9 us: block_terms(): first = jnp.dot(strength, cosine, precision=lax.Precision.HIGHEST)]
    add x1 -> x0, other arithmetic: 18 us -> none  [block_terms(): first[:half] + second[half:]]
    concatenate x1 -> x0, other arithmetic: 11.6 us -> none  [block_terms(): jnp.concatenate([first[:half] + second[half:], first[half:] - second[:hal...]
    all_gather x1 -> x0, blocking collectives: 11.2 us -> none  [local(): lax.all_gather(coords, 'dir', axis=1, tiled=True)]
  transfers between devices with their start and end apart: 2 -> 0, of which waited for: 1 -> 0; matrix products, arithmetic and copies ran while one was open for 35% -> 0% of each run, Pallas kernels for 0% -> 0%
where the time goes in v1:
time: 90.2 us; the launch traced here: 90 us
  Pallas kernels  87 us (96%)
  local copies, waits for them, and re-layouts  2.37 us (3%)
    pallas_call x1, Pallas kernels, local(): pl.pallas_call(kernel, out_shape=jax.ShapeDtypeStruct((512, BLK), F32), i...  87 us
    broadcast_in_dim x1, local copies, waits for them, and re-layouts, local(): return out[:, None, :]  2.37 us

profile of v1, /device:TPU:1, one launch (start us, length us, event | category | flops | bytes accessed | tf_op | source)
XLA Modules:
  0.0 90.0 jit_solution(3611643490941162114)
XLA Ops:
  0.7 87.0 %far_field.1 = f32[512,256]{1,0:T(8,128)} custom-call(f32[512,256]{1,0:T(8,128)} %dens.1, f32[1,256]{1,0:T(1,128)} %bitcast.3, f32[3,256]{1,0:T(4,128)} %coords.1, s32[1]{0:T(128)S(6)} %copy.7.counts, f32[3,1,8192]{2,1,0:T(1,128)} %wave.1), custom_call_target="tpu_custom_call" | custom-call | flops 8600000512 | bytes 2000000 | tf_op jit(solution)/shard_map/far_field/pallas_call | solution.py:329
  87.7 2.4 %copy.6 = f32[512,1,256]{2,1,0:T(1,128)} copy(f32[512,1,256]{2,0,1:T(8,128)} %bitcast.2) | data formatting | bytes 1048576 | tf_op jit(solution)/shard_map/broadcast_in_dim | solution.py:371

commit v2 on v1

v2 whole, which is shorter than its diff:
```python
import functools
import math

import numpy as np

import jax
import jax.numpy as jnp
from jax import lax
from jax.experimental import pallas as pl
from jax.experimental.pallas import tpu as pltpu
from jax.sharding import PartitionSpec as P

MESH = pl.DeviceIdType.MESH
F32, BF16, I32 = jnp.float32, jnp.bfloat16, jnp.int32
N = 4
PTS = 128
NCH = 4
HB = 64
NDIR = 2048
BLK = 256


def _fit(f, terms, odd):
    x = np.cos(np.linspace(0, np.pi / 2, 2001)) * 0.5
    a = np.stack([x ** (2 * k + odd) for k in range(terms)], 1)
    w = np.ones_like(x)
    for _ in range(60):
        c = np.linalg.lstsq(a * w[:, None], f(x) * w, rcond=None)[0]
        e = np.abs(a @ c - f(x))
        w = w * np.sqrt(e / e.max() + 0.02)
        w = w / w.max()
    return [float(np.float32(v)) for v in c * math.sqrt(2.0)]


SIN = _fit(lambda r: np.sin(np.pi * r), 3, 1)
COS = _fit(lambda r: np.cos(np.pi * r), 4, 0)


def horner(q, c):
    acc = c[-1] * q + c[-2]
    for k in c[-3::-1]:
        acc = acc * q + k
    return acc


def split3(v):
    a = v.astype(BF16).astype(F32)
    b = (v - a).astype(BF16).astype(F32)
    return a, b, (v - a) - b


E_STEPS = {
    1: [(0, 0)], 2: [(1, 0)], 3: [(2, 0)], 4: [(0, 1), (3, 0)], 5: [(1, 1)], 6: [(0, 2), (2, 1)], 7: [(3, 1)], 8: [(1, 2)],
    11: [(0, 3)], 12: [(2, 2)], 14: [(1, 3)], 15: [(0, 4), (3, 2)],
}
M_STEPS = {2: [(2, 3)], 3: [(1, 4)], 6: [(3, 3)], 7: [(2, 4)], 11: [(3, 4)]}


def kernel(
    dens_h, wts_h, coords_h, counts, wave_h, out,
    dens, wts, coords, wave, W, cnt1, cnt2, raw, shv, cnv, kf, kmat, X, keep, sout, sin_, G, E0, E1, E2, E3, L, Pm, Po, Cx,
    Hp, Hm, Rp, Rm,
    ins, s1s, s1r, s2s, s2r, sgs, sgr, sxs, sxr, shs, shr, ggs, ggr, cxs, cxr, hs, hr, rs, rr,
):
    E = (E0, E1, E2, E3)
    surf, z = lax.axis_index("surf"), lax.axis_index("dir")
    x, y, c = surf // 8, (surf // 2) % N, surf % 2
    q = surf * N + z

    def dev(xx, yy, cc, zz):
        return ((xx * N + yy) * 2 + cc, zz)

    def up(v, k):
        return lax.rem(v + (k + N), N)

    def remote(src, dst, ss, rs_, to):
        return pltpu.make_async_remote_copy(
            src_ref=src, dst_ref=dst, send_sem=ss, recv_sem=rs_, device_id=to, device_id_type=MESH
        )

    me8 = c * N + z
    peers8 = []
    for k in range(1, 8):
        o = lax.rem(me8 + k, 8)
        peers8.append(dev(x, y, o // N, lax.rem(o, N)))
    peers16 = [dev(up(x, i), up(y, j), c, z) for i in range(N) for j in range(N) if i or j]
    peersyz = [(i, j) for i in range(N) for j in range(N) if i or j]
    qn = lax.rem(q + 1, 128)
    nxt = (qn // N, lax.rem(qn, N))
    run = lax.rem(surf + 1, 32)
    runx, runy, runc = run // 8, (run // 2) % N, run % 2
    group = [dev(runx, i, runc, j) for i in range(N) for j in range(N)]
    ends = [(lax.rem((x * N + i) * 2 + c + 31, 32), N - 1) for i in range(N)]

    barrier = pltpu.get_barrier_semaphore()
    extra = [dev(x, up(y, i), c, up(z, j)) for i, j in peersyz if i and j]
    greet = peers8 + peers16 + extra + ends
    heard = len(greet) - N + jnp.where(z == N - 1, N * N, 0)
    for to in greet:
        pl.semaphore_signal(barrier, inc=1, device_id=to, device_id_type=MESH)
    fetch = [
        pltpu.make_async_copy(a, b, ins.at[k])
        for k, (a, b) in enumerate(((dens_h, dens), (wts_h, wts), (coords_h, coords), (wave_h, wave)))
    ]
    for d in fetch:
        d.start()
    cnt = counts[0]
    own = y * N + z
    raw[own] = jnp.zeros((8, 256), F32)
    cnt1[me8] = jnp.full((8, 128), cnt, I32)
    pl.semaphore_wait(barrier, heard)

    n1 = [
        remote(cnt1.at[me8], cnt1.at[me8], s1s.at[k], s1r.at[k], peers8[k]) for k in range(7)
    ]
    for d in n1:
        d.start()

    for d in fetch:
        d.wait()
    scale = 1.0 / math.sqrt(PTS * 128)
    w = wts[...]
    for ch in range(NCH):
        W[ch, 0:HB] = ((w * dens[ch * HB : (ch + 1) * HB, :]) * scale).astype(BF16)
        W[ch, HB:] = ((w * dens[256 + ch * HB : 256 + (ch + 1) * HB, :]) * scale).astype(BF16)
    kf[...] = jnp.zeros_like(kf)
    for t, dx in enumerate((2, 1, 3, 0)):
        for h in range(2):
            cc = c if h == 0 else 1 - c
            at = pl.multiple_of((up(x, dx) * 8 + y * 2 + cc) * BLK, BLK)
            for k in range(3):
                kf[k : k + 1, t * 512 + h * BLK : t * 512 + (h + 1) * BLK] = (
                    wave[k, :, pl.ds(at, BLK)] * (1.0 / (2.0 * math.pi))
                )
    k1, k2, k3 = split3(kf[...])
    kmat[...] = jnp.concatenate([k1, k2, k1, k3, k2, k1, jnp.zeros((80, NDIR), F32)], 0).astype(BF16)

    for d in n1:
        d.wait_recv()
    eight = jnp.zeros((8, 128), I32)
    line = lax.broadcasted_iota(I32, (8, 128), 0)
    for k in range(8):
        eight = jnp.where(line == k, cnt1[k], eight)
    me16 = x * N + y
    cnt2[me16] = eight
    n2 = [
        remote(cnt2.at[me16], cnt2.at[me16], s2s.at[k], s2r.at[k], peers16[k]) for k in range(15)
    ]
    for d in n2:
        d.start()

    raw[own, 0:3] = coords[...]
    dg = [
        remote(raw.at[own], raw.at[own], sgs.at[k], sgr.at[k], dev(x, up(y, i), c, up(z, j)))
        for k, (i, j) in enumerate(peersyz)
    ]
    for d in dg:
        d.start()

    def end_copy(k):
        return remote(raw.at[own], raw.at[16 + runy], sxs.at[k], sxr.at[runy], group[k])

    @pl.when(z == N - 1)
    def _():
        for k in range(16):
            end_copy(k).start()

    for d in n2:
        d.wait_recv()
    nums = cnt2[...].reshape(128, 128).astype(F32)
    at_row = lax.broadcasted_iota(I32, (128, 128), 0)
    at_col = lax.broadcasted_iota(I32, (128, 128), 1)
    lower = jnp.where(at_col < at_row, 1.0, 0.0).astype(BF16)
    cnv[...] = nums
    shv[...] = jnp.dot(lower, nums.astype(BF16), preferred_element_type=F32) - (at_row * PTS).astype(F32)

    def wide(row):
        return jnp.concatenate([row, row], 1)

    slot = lax.broadcasted_iota(I32, (256, 256), 0).astype(F32)
    col = lax.broadcasted_iota(I32, (256, 256), 1).astype(F32)
    myshift, mycnt = wide(shv[pl.ds(q, 1), :]), wide(cnv[pl.ds(q, 1), :])
    pick = jnp.where((col - slot == myshift) & (slot < mycnt), 1.0, 0.0).astype(BF16)

    dsh = [remote(sout.at[ch], sin_.at[ch], shs.at[ch], shr.at[ch], nxt) for ch in range(NCH)]

    def pack(ch):
        moved = jnp.dot(W[ch], pick, preferred_element_type=F32)
        keep[ch] = moved[:, :128]
        sout[ch] = moved[:, 128:]
        dsh[ch].start()

    for ch in range(NCH):
        pack(ch)

    def gcopies(ch, st):
        sem = lambda n: (ggs.at[ch, st * 4 + n], ggr.at[ch, st * 4 + n])
        yn, yp, zn, zp = (dev(x, up(y, 1), c, z), dev(x, up(y, -1), c, z), dev(x, y, c, up(z, 1)), dev(x, y, c, up(z, -1)))
        ym, yq, zm, zq = up(y, -1), up(y, 1), up(z, -1), up(z, 1)
        lo, lo1, lo2 = pl.ds(0, 64), pl.ds(0, 32), pl.ds(32, 32)
        hi, hi1, hi2 = pl.ds(64, 64), pl.ds(64, 32), pl.ds(96, 32)
        al = pl.ds(0, N)
        if st == 0:
            parts = [((y, z, lo), yn), ((y, z, lo), yp), ((y, z, hi), zn), ((y, z, hi), zp)]
        elif st == 1:
            parts = [((ym, z, lo1), yn), ((yq, z, lo2), yp), ((y, zm, hi1), zn), ((y, zq, hi2), zp)]
        elif st == 2:
            parts = [((al, z, lo), zn), ((al, z, lo), zp), ((y, al, hi), yn), ((y, al, hi), yp)]
        else:
            parts = [((al, zm, lo1), zn), ((al, zq, lo2), zp), ((ym, al, hi1), yn), ((yq, al, hi2), yp)]
        return [remote(G.at[(ch,) + p], G.at[(ch,) + p], *sem(n), to) for n, (p, to) in enumerate(parts)]

    def gstep(ch, st):
        if st == 0:
            dsh[ch].wait_recv()
            G[ch, y, z] = keep[ch] + sin_[ch]
        else:
            for d in gcopies(ch, st - 1):
                d.wait_recv()
        if st < 4:
            for d in gcopies(ch, st):
                d.start()

    for d in dg:
        d.wait_recv()
    for k in range(N):
        remote(raw.at[own], raw.at[16 + k], sxs.at[k], sxr.at[k], group[0]).wait_recv()

    slot_l = lax.broadcasted_iota(I32, (PTS, 256), 1).astype(F32)
    pos = lax.broadcasted_iota(I32, (PTS, 256), 0).astype(F32)

    def terms(k):
        a1, a2, a3 = split3(raw[k])
        return jnp.concatenate([a1, a1, a2, a1, a2, a3, jnp.zeros((80, 256), F32)], 0).astype(BF16)

    def chosen(dev_q, first):
        off, num = wide(shv[pl.ds(dev_q, 1), :]), wide(cnv[pl.ds(dev_q, 1), :])
        return jnp.where((pos + first - slot_l == off) & (slot_l < num), 1.0, 0.0).astype(BF16)

    def placed(yy, zz):
        qb = ((x * N + yy) * 2 + c) * N + zz
        ahead = 16 + yy if zz == 0 else yy * N + zz - 1
        dims = (((1,), (1,)), ((), ()))
        kept = lax.dot_general(chosen(qb, 0.0), terms(yy * N + zz), dims, preferred_element_type=F32)
        came = lax.dot_general(
            chosen(lax.rem(qb + 127, 128), 128.0), terms(ahead), dims, preferred_element_type=F32
        )
        return (kept + came).astype(BF16)

    def waves(t, i):
        yy = up(y, i)
        for h in range(2):
            rows = pl.multiple_of(yy * 512 + h * 256, 256)
            if t == 0:
                for k in range(2):
                    X[pl.ds(pl.multiple_of(rows + k * PTS, PTS), PTS), :] = placed(yy, h * 2 + k)
            xm = X[pl.ds(rows, 256), :]
            for j in range(2):
                cols = slice(j * 256, (j + 1) * 256)
                turn = jnp.dot(xm, kmat[:, t * 512 + j * 256 : t * 512 + (j + 1) * 256], preferred_element_type=F32)
                r = turn - jnp.round(turn)
                r2 = r * r
                s = r * horner(r2, SIN)
                E[t][pl.ds(rows, 256), cols] = (1.0 - s * s).astype(BF16)
                E[t][pl.ds(pl.multiple_of(rows + 2048, 256), 256), cols] = (s * horner(r2, COS)).astype(BF16)

    def wave_loop(t):
        @pl.loop(0, 4)
        def _(i):
            waves(t, i)
            for k in range(4):
                steps = E_STEPS.get(t * 4 + k, [])
                if steps:
                    @pl.when(i == k)
                    def _():
                        for ch, st in steps:
                            gstep(ch, st)

    xn, xp, other = dev(up(x, 1), y, c, z), dev(up(x, -1), y, c, z), dev(x, y, 1 - c, z)

    def core_copy(ch, t):
        m = ch * 4 + t
        return remote(Po.at[m], Cx.at[m], cxs.at[m], cxr.at[m], other)

    def half_copy(ch, n):
        land, to = ((Hp, xn), (Hm, xp))[n]
        k = n * NCH + ch
        return remote(Pm.at[ch * 4, pl.ds(64 * n, 64)], land.at[ch], hs.at[k], hr.at[k], to)

    def full_copy(ch, n):
        land, to = ((Rp, xn), (Rm, xp))[n]
        k = n * NCH + ch
        return remote(Pm.at[ch * 4 + 1 + n], land.at[ch], rs.at[k], rr.at[k], to)

    def core_done(ch, t):
        core_copy(ch, t).wait_recv()
        m = ch * 4 + t
        Pm[m] = Pm[m] + Cx[m]
        if t == 0:
            half_copy(ch, 0).start()
            half_copy(ch, 1).start()

    def forward(ch):
        for n in range(2):
            half_copy(ch, n).wait_recv()
            here = pl.ds(64 * n, 64)
            Pm[ch * 4 + 1 + n, here] = Pm[ch * 4 + 1 + n, here] + (Hp, Hm)[n][ch]
            full_copy(ch, n).start()

    def finish(ch):
        full_copy(ch, 0).wait_recv()
        full_copy(ch, 1).wait_recv()
        res = Pm[ch * 4 + 3] + Rp[ch] + Rm[ch]
        out[pl.ds(pl.multiple_of(ch * HB, HB), HB), :] = res[0:64]
        out[pl.ds(pl.multiple_of(256 + ch * HB, HB), HB), :] = res[64:128]

    def build(ch):
        for b in range(16):
            g = G[ch, b // N, b % N]
            lo, hi = g[0:64].astype(BF16), g[64:128].astype(BF16)
            cols, cols2 = slice(b * PTS, (b + 1) * PTS), slice(2048 + b * PTS, 2048 + (b + 1) * PTS)
            L[0:64, cols] = lo
            L[0:64, cols2] = hi
            L[64:128, cols] = hi
            L[64:128, cols2] = -lo

    def product(ch, t):
        part = jnp.dot(L[...], E[t][...], preferred_element_type=F32)
        Pm[ch * 4 + t] = part[:, :BLK]
        Po[ch * 4 + t] = part[:, BLK:]
        core_copy(ch, t).start()

    def m_steps(m):
        for ch, st in M_STEPS.get(m, []):
            gstep(ch, st)

    for t in range(4):
        wave_loop(t)

    @pl.loop(0, NCH)
    def _(ch):
        build(ch)
        for t in range(4):
            product(ch, t)
            if t < 2:
                @pl.when(ch > 0)
                def _():
                    core_done(ch - 1, t + 2)
            else:
                core_done(ch, t - 2)
            if t == 2:
                @pl.when(ch > 0)
                def _():
                    forward(ch - 1)
            for k in range(NCH):
                if k * 4 + t in M_STEPS:
                    @pl.when(ch == k)
                    def _():
                        m_steps(k * 4 + t)

    core_done(NCH - 1, 2)
    core_done(NCH - 1, 3)
    forward(NCH - 1)
    for ch in range(NCH):
        finish(ch)

    for d in n1 + n2 + dsh + dg:
        d.wait_send()

    @pl.when(z == N - 1)
    def _():
        for k in range(16):
            end_copy(k).wait_send()

    for ch in range(NCH):
        for st in range(4):
            for d in gcopies(ch, st):
                d.wait_send()
        for n in range(2):
            half_copy(ch, n).wait_send()
            full_copy(ch, n).wait_send()
        for t in range(4):
            core_copy(ch, t).wait_send()


def local(densities, weights, coords, counts, wave):
    vm, hbm = pl.BlockSpec(memory_space=pltpu.VMEM), pl.BlockSpec(memory_space=pl.ANY)
    dma = pltpu.SemaphoreType.DMA
    out = pl.pallas_call(
        kernel,
        out_shape=jax.ShapeDtypeStruct((512, BLK), F32),
        in_specs=[hbm, hbm, hbm, pl.BlockSpec(memory_space=pltpu.SMEM), hbm],
        out_specs=vm,
        scratch_shapes=[
            pltpu.VMEM((512, 256), F32),
            pltpu.VMEM((1, 256), F32),
            pltpu.VMEM((3, 256), F32),
            pltpu.VMEM((3, 1, 8192), F32),
            pltpu.VMEM((NCH, 128, 256), BF16),
            pltpu.VMEM((8, 8, 128), I32),
            pltpu.VMEM((16, 8, 128), I32),
            pltpu.VMEM((20, 8, 256), F32),
            pltpu.VMEM((128, 128), F32),
            pltpu.VMEM((128, 128), F32),
            pltpu.VMEM((8, NDIR), F32),
            pltpu.VMEM((128, NDIR), BF16),
            pltpu.VMEM((2048, 128), BF16),
            pltpu.VMEM((NCH, 128, 128), F32),
            pltpu.VMEM((NCH, 128, 128), F32),
            pltpu.VMEM((NCH, 128, 128), F32),
            pltpu.VMEM((NCH, N, N, 128, 128), F32),
            pltpu.VMEM((4096, 512), BF16),
            pltpu.VMEM((4096, 512), BF16),
            pltpu.VMEM((4096, 512), BF16),
            pltpu.VMEM((4096, 512), BF16),
            pltpu.VMEM((128, 4096), BF16),
            pltpu.VMEM((16, 128, BLK), F32),
            pltpu.VMEM((16, 128, BLK), F32),
            pltpu.VMEM((16, 128, BLK), F32),
            pltpu.VMEM((NCH, 64, BLK), F32),
            pltpu.VMEM((NCH, 64, BLK), F32),
            pltpu.VMEM((NCH, 128, BLK), F32),
            pltpu.VMEM((NCH, 128, BLK), F32),
            dma((4,)),
            dma((7,)), dma((7,)),
            dma((15,)), dma((15,)),
            dma((15,)), dma((15,)),
            dma((16,)), dma((N,)),
            dma((NCH,)), dma((NCH,)),
            dma((NCH, 16)), dma((NCH, 16)),
            dma((16,)), dma((16,)),
            dma((2 * NCH,)), dma((2 * NCH,)),
            dma((2 * NCH,)), dma((2 * NCH,)),
        ],
        compiler_params=pltpu.CompilerParams(
            collective_id=0, has_side_effects=True, vmem_limit_bytes=56 * 2**20
        ),
        cost_estimate=pl.CostEstimate(flops=8_600_000_000, bytes_accessed=2_000_000, transcendentals=0),
        name="far_field",
    )(densities, weights.reshape(1, -1), coords, counts, wave)
    return out[:, None, :]


def solution(mesh):
    placed = (
        P(None, ("surf", "dir")),
        P(("surf", "dir")),
        P(None, ("surf", "dir")),
        P(("surf", "dir")),
        P(None, "dir", None),
    )
    return jax.shard_map(
        local, mesh=mesh, in_specs=placed, out_specs=P(None, "dir", "surf"), check_vma=False
    )
```

time: 90.2 us -> 71.6 us (0.79)
  Pallas kernels: 87 us -> 68.4 us
    pallas_call x1, Pallas kernels: 87 us -> 68.4 us  [local(): pl.pallas_call(kernel, out_shape=jax.ShapeDtypeStruct((512, BLK), F32), i...]
where the time goes in v2:
time: 71.6 us; the launch traced here: 71.4 us
  Pallas kernels  68.4 us (96%)
  local copies, waits for them, and re-layouts  2.37 us (3%)
    pallas_call x1, Pallas kernels, local(): pl.pallas_call(kernel, out_shape=jax.ShapeDtypeStruct((512, BLK), F32), i...  68.4 us
    broadcast_in_dim x1, local copies, waits for them, and re-layouts, local(): return out[:, None, :]  2.37 us

profile of v2, /device:TPU:1, one launch (start us, length us, event | category | flops | bytes accessed | tf_op | source)
XLA Modules:
  0.0 71.4 jit_solution(17925595696385700675)
XLA Ops:
  0.7 68.4 %far_field.1 = f32[512,256]{1,0:T(8,128)} custom-call(f32[512,256]{1,0:T(8,128)} %dens_h.1, f32[1,256]{1,0:T(1,128)} %bitcast.3, f32[3,256]{1,0:T(4,128)} %coords_h.1, s32[1]{0:T(128)S(6)} %copy.7.counts, f32[3,1,8192]{2,1,0:T(1,128)} %wave_h.1), custom_call_target="tpu_custom_call" | custom-call | flops 8600000512 | bytes 2000000 | tf_op jit(solution)/shard_map/far_field/pallas_call | solution.py:389
  69.1 2.4 %copy.6 = f32[512,1,256]{2,1,0:T(1,128)} copy(f32[512,1,256]{2,0,1:T(8,128)} %bitcast.2) | data formatting | bytes 1048576 | tf_op jit(solution)/shard_map/broadcast_in_dim | solution.py:441

commit v3 on v2

--- a/solution.py
+++ b/solution.py
@@ -58,11 +58,10 @@
 
 def kernel(
     dens_h, wts_h, coords_h, counts, wave_h, out,
-    dens, wts, coords, wave, W, cnt1, cnt2, raw, shv, cnv, kf, kmat, X, keep, sout, sin_, G, E0, E1, E2, E3, L, Pm, Po, Cx,
+    dens, wts, coords, wave, W, cnt1, cnt2, raw, shv, cnv, kf, kmat, X, keep, sout, sin_, G, E, L, Pm, Po, Cx,
     Hp, Hm, Rp, Rm,
     ins, s1s, s1r, s2s, s2r, sgs, sgr, sxs, sxr, shs, shr, ggs, ggr, cxs, cxr, hs, hr, rs, rr,
 ):
-    E = (E0, E1, E2, E3)
     surf, z = lax.axis_index("surf"), lax.axis_index("dir")
     x, y, c = surf // 8, (surf // 2) % N, surf % 2
     q = surf * N + z
@@ -90,12 +89,9 @@
     run = lax.rem(surf + 1, 32)
     runx, runy, runc = run // 8, (run // 2) % N, run % 2
     group = [dev(runx, i, runc, j) for i in range(N) for j in range(N)]
-    ends = [(lax.rem((x * N + i) * 2 + c + 31, 32), N - 1) for i in range(N)]
 
     barrier = pltpu.get_barrier_semaphore()
-    extra = [dev(x, up(y, i), c, up(z, j)) for i, j in peersyz if i and j]
-    greet = peers8 + peers16 + extra + ends
-    heard = len(greet) - N + jnp.where(z == N - 1, N * N, 0)
+    greet = peers8 + peers16
     for to in greet:
         pl.semaphore_signal(barrier, inc=1, device_id=to, device_id_type=MESH)
     fetch = [
@@ -108,7 +104,7 @@
     own = y * N + z
     raw[own] = jnp.zeros((8, 256), F32)
     cnt1[me8] = jnp.full((8, 128), cnt, I32)
-    pl.semaphore_wait(barrier, heard)
+    pl.semaphore_wait(barrier, len(greet))
 
     n1 = [
         remote(cnt1.at[me8], cnt1.at[me8], s1s.at[k], s1r.at[k], peers8[k]) for k in range(7)
@@ -133,7 +129,9 @@
                     wave[k, :, pl.ds(at, BLK)] * (1.0 / (2.0 * math.pi))
                 )
     k1, k2, k3 = split3(kf[...])
-    kmat[...] = jnp.concatenate([k1, k2, k1, k3, k2, k1, jnp.zeros((80, NDIR), F32)], 0).astype(BF16)
+    turns = jnp.concatenate([k1, k2, k1, k3, k2, k1, jnp.zeros((80, NDIR), F32)], 0).astype(BF16)
+    for t in range(4):
+        kmat[t] = turns[:, t * 512 : (t + 1) * 512]
 
     for d in n1:
         d.wait_recv()
@@ -239,7 +237,7 @@
 
     def placed(yy, zz):
         qb = ((x * N + yy) * 2 + c) * N + zz
-        ahead = 16 + yy if zz == 0 else yy * N + zz - 1
+        ahead = jnp.where(zz == 0, 16 + yy, yy * N + zz - 1)
         dims = (((1,), (1,)), ((), ()))
         kept = lax.dot_general(chosen(qb, 0.0), terms(yy * N + zz), dims, preferred_element_type=F32)
         came = lax.dot_general(
@@ -247,34 +245,30 @@
         )
         return (kept + came).astype(BF16)
 
-    def waves(t, i):
-        yy = up(y, i)
+    @pl.loop(0, 16)
+    def _(b):
+        yy, zz = b // N, lax.rem(b, N)
+        X[pl.ds(pl.multiple_of(b * PTS, PTS), PTS), :] = placed(yy, zz)
+
+    @pl.loop(0, 16)
+    def _(it):
+        t, i = it // 4, lax.rem(it, 4)
         for h in range(2):
-            rows = pl.multiple_of(yy * 512 + h * 256, 256)
-            if t == 0:
-                for k in range(2):
-                    X[pl.ds(pl.multiple_of(rows + k * PTS, PTS), PTS), :] = placed(yy, h * 2 + k)
+            rows = pl.multiple_of(i * 512 + h * 256, 256)
             xm = X[pl.ds(rows, 256), :]
             for j in range(2):
                 cols = slice(j * 256, (j + 1) * 256)
-                turn = jnp.dot(xm, kmat[:, t * 512 + j * 256 : t * 512 + (j + 1) * 256], preferred_element_type=F32)
+                turn = jnp.dot(xm, kmat[t, :, cols], preferred_element_type=F32)
                 r = turn - jnp.round(turn)
                 r2 = r * r
                 s = r * horner(r2, SIN)
-                E[t][pl.ds(rows, 256), cols] = (1.0 - s * s).astype(BF16)
-                E[t][pl.ds(pl.multiple_of(rows + 2048, 256), 256), cols] = (s * horner(r2, COS)).astype(BF16)
-
-    def wave_loop(t):
-        @pl.loop(0, 4)
-        def _(i):
-            waves(t, i)
-            for k in range(4):
-                steps = E_STEPS.get(t * 4 + k, [])
-                if steps:
-                    @pl.when(i == k)
-                    def _():
-                        for ch, st in steps:
-                            gstep(ch, st)
+                E[t, pl.ds(rows, 256), cols] = (1.0 - s * s).astype(BF16)
+                E[t, pl.ds(pl.multiple_of(rows + 2048, 256), 256), cols] = (s * horner(r2, COS)).astype(BF16)
+        for k, steps in E_STEPS.items():
+            @pl.when(it == k)
+            def _():
+                for ch, st in steps:
+                    gstep(ch, st)
 
     xn, xp, other = dev(up(x, 1), y, c, z), dev(up(x, -1), y, c, z), dev(x, y, 1 - c, z)
 
@@ -325,7 +319,7 @@
             L[64:128, cols2] = -lo
 
     def product(ch, t):
-        part = jnp.dot(L[...], E[t][...], preferred_element_type=F32)
+        part = jnp.dot(L[...], E[t], preferred_element_type=F32)
         Pm[ch * 4 + t] = part[:, :BLK]
         Po[ch * 4 + t] = part[:, BLK:]
         core_copy(ch, t).start()
@@ -334,29 +328,27 @@
         for ch, st in M_STEPS.get(m, []):
             gstep(ch, st)
 
-    for t in range(4):
-        wave_loop(t)
-
-    @pl.loop(0, NCH)
-    def _(ch):
-        build(ch)
-        for t in range(4):
-            product(ch, t)
-            if t < 2:
-                @pl.when(ch > 0)
-                def _():
-                    core_done(ch - 1, t + 2)
-            else:
-                core_done(ch, t - 2)
-            if t == 2:
-                @pl.when(ch > 0)
-                def _():
-                    forward(ch - 1)
-            for k in range(NCH):
-                if k * 4 + t in M_STEPS:
-                    @pl.when(ch == k)
+    @pl.loop(0, 4 * NCH)
+    def _(m):
+        ch, t = m // 4, lax.rem(m, 4)
+
+        @pl.when(t == 0)
+        def _():
+            build(ch)
+
+        product(ch, t)
+        for k in range(4):
+            @pl.when((t == k) & (m > 1))
+            def _():
+                core_done(ch - (1 if k < 2 else 0), (k + 2) % 4)
+                if k == 2:
+                    @pl.when(ch > 0)
                     def _():
-                        m_steps(k * 4 + t)
+                        forward(ch - 1)
+        for k in M_STEPS:
+            @pl.when(m == k)
+            def _():
+                m_steps(k)
 
     core_done(NCH - 1, 2)
     core_done(NCH - 1, 3)
@@ -403,16 +395,13 @@
             pltpu.VMEM((128, 128), F32),
             pltpu.VMEM((128, 128), F32),
             pltpu.VMEM((8, NDIR), F32),
-            pltpu.VMEM((128, NDIR), BF16),
+            pltpu.VMEM((4, 128, 512), BF16),
             pltpu.VMEM((2048, 128), BF16),
             pltpu.VMEM((NCH, 128, 128), F32),
             pltpu.VMEM((NCH, 128, 128), F32),
             pltpu.VMEM((NCH, 128, 128), F32),
             pltpu.VMEM((NCH, N, N, 128, 128), F32),
-            pltpu.VMEM((4096, 512), BF16),
-            pltpu.VMEM((4096, 512), BF16),
-            pltpu.VMEM((4096, 512), BF16),
-            pltpu.VMEM((4096, 512), BF16),
+            pltpu.VMEM((4, 4096, 512), BF16),
             pltpu.VMEM((128, 4096), BF16),
             pltpu.VMEM((16, 128, BLK), F32),
             pltpu.VMEM((16, 128, BLK), F32),

time: 71.6 us -> 70.8 us (0.989)
  Pallas kernels: 68.4 us -> 67.6 us
    pallas_call x1, Pallas kernels: 68.4 us -> 67.6 us  [local(): pl.pallas_call(kernel, out_shape=jax.ShapeDtypeStruct((512, BLK), F32), i...]
where the time goes in v3:
time: 70.8 us; the launch traced here: 70.7 us
  Pallas kernels  67.6 us (95%)
  local copies, waits for them, and re-layouts  2.37 us (3%)
    pallas_call x1, Pallas kernels, local(): pl.pallas_call(kernel, out_shape=jax.ShapeDtypeStruct((512, BLK), F32), i...  67.6 us
    broadcast_in_dim x1, local copies, waits for them, and re-layouts, local(): return out[:, None, :]  2.37 us

profile of v3, /device:TPU:1, one launch (start us, length us, event | category | flops | bytes accessed | tf_op | source)
XLA Modules:
  0.0 70.7 jit_solution(15053963349641626977)
XLA Ops:
  0.7 67.6 %far_field.1 = f32[512,256]{1,0:T(8,128)} custom-call(f32[512,256]{1,0:T(8,128)} %dens_h.1, f32[1,256]{1,0:T(1,128)} %bitcast.3, f32[3,256]{1,0:T(4,128)} %coords_h.1, s32[1]{0:T(128)S(6)} %copy.7.counts, f32[3,1,8192]{2,1,0:T(1,128)} %wave_h.1), custom_call_target="tpu_custom_call" | custom-call | flops 8600000512 | bytes 2000000 | tf_op jit(solution)/shard_map/far_field/pallas_call | solution.py:381
  68.3 2.4 %copy.6 = f32[512,1,256]{2,1,0:T(1,128)} copy(f32[512,1,256]{2,0,1:T(8,128)} %bitcast.2) | data formatting | bytes 1048576 | tf_op jit(solution)/shard_map/broadcast_in_dim | solution.py:430

commit v4 on v3

--- a/solution.py
+++ b/solution.py
@@ -49,11 +49,8 @@
     return a, b, (v - a) - b
 
 
-E_STEPS = {
-    1: [(0, 0)], 2: [(1, 0)], 3: [(2, 0)], 4: [(0, 1), (3, 0)], 5: [(1, 1)], 6: [(0, 2), (2, 1)], 7: [(3, 1)], 8: [(1, 2)],
-    11: [(0, 3)], 12: [(2, 2)], 14: [(1, 3)], 15: [(0, 4), (3, 2)],
-}
-M_STEPS = {2: [(2, 3)], 3: [(1, 4)], 6: [(3, 3)], 7: [(2, 4)], 11: [(3, 4)]}
+E_STEPS = {1: [(0, 0)], 2: [(1, 0)], 3: [(2, 0)], 4: [(3, 0)], 5: [(0, 1)], 7: [(1, 1)], 10: [(0, 2)], 11: [(2, 1)], 13: [(1, 2)], 14: [(3, 1)], 15: [(0, 3)]}
+M_STEPS = {2: [(2, 2)], 3: [(1, 3)], 6: [(3, 2)], 7: [(2, 3)], 11: [(3, 3)]}
 
 
 def kernel(
@@ -192,21 +189,23 @@
         pack(ch)
 
     def gcopies(ch, st):
-        sem = lambda n: (ggs.at[ch, st * 4 + n], ggr.at[ch, st * 4 + n])
-        yn, yp, zn, zp = (dev(x, up(y, 1), c, z), dev(x, up(y, -1), c, z), dev(x, y, c, up(z, 1)), dev(x, y, c, up(z, -1)))
+        yn, yp, yo = (dev(x, up(y, k), c, z) for k in (1, -1, 2))
+        zn, zp, zo = (dev(x, y, c, up(z, k)) for k in (1, -1, 2))
         ym, yq, zm, zq = up(y, -1), up(y, 1), up(z, -1), up(z, 1)
         lo, lo1, lo2 = pl.ds(0, 64), pl.ds(0, 32), pl.ds(32, 32)
         hi, hi1, hi2 = pl.ds(64, 64), pl.ds(64, 32), pl.ds(96, 32)
         al = pl.ds(0, N)
         if st == 0:
-            parts = [((y, z, lo), yn), ((y, z, lo), yp), ((y, z, hi), zn), ((y, z, hi), zp)]
+            mine, yours = (y, z, lo), (y, z, hi)
+            parts = [(mine, yn), (mine, yp), (yours, zn), (yours, zp), (mine, yo), (yours, zo)]
         elif st == 1:
-            parts = [((ym, z, lo1), yn), ((yq, z, lo2), yp), ((y, zm, hi1), zn), ((y, zq, hi2), zp)]
-        elif st == 2:
             parts = [((al, z, lo), zn), ((al, z, lo), zp), ((y, al, hi), yn), ((y, al, hi), yp)]
         else:
             parts = [((al, zm, lo1), zn), ((al, zq, lo2), zp), ((ym, al, hi1), yn), ((yq, al, hi2), yp)]
-        return [remote(G.at[(ch,) + p], G.at[(ch,) + p], *sem(n), to) for n, (p, to) in enumerate(parts)]
+        return [
+            remote(G.at[(ch,) + p], G.at[(ch,) + p], ggs.at[ch, st * 6 + n], ggr.at[ch, st * 6 + n], to)
+            for n, (p, to) in enumerate(parts)
+        ]
 
     def gstep(ch, st):
         if st == 0:
@@ -215,7 +214,7 @@
         else:
             for d in gcopies(ch, st - 1):
                 d.wait_recv()
-        if st < 4:
+        if st < 3:
             for d in gcopies(ch, st):
                 d.start()
 
@@ -351,8 +350,8 @@
                 m_steps(k)
 
     core_done(NCH - 1, 2)
+    forward(NCH - 1)
     core_done(NCH - 1, 3)
-    forward(NCH - 1)
     for ch in range(NCH):
         finish(ch)
 
@@ -365,7 +364,7 @@
             end_copy(k).wait_send()
 
     for ch in range(NCH):
-        for st in range(4):
+        for st in range(3):
             for d in gcopies(ch, st):
                 d.wait_send()
         for n in range(2):
@@ -416,7 +415,7 @@
             dma((15,)), dma((15,)),
             dma((16,)), dma((N,)),
             dma((NCH,)), dma((NCH,)),
-            dma((NCH, 16)), dma((NCH, 16)),
+            dma((NCH, 18)), dma((NCH, 18)),
             dma((16,)), dma((16,)),
             dma((2 * NCH,)), dma((2 * NCH,)),
             dma((2 * NCH,)), dma((2 * NCH,)),

time: 70.8 us -> 69.6 us (0.983)
  Pallas kernels: 67.6 us -> 66.5 us
    pallas_call x1, Pallas kernels: 67.6 us -> 66.5 us  [local(): pl.pallas_call(kernel, out_shape=jax.ShapeDtypeStruct((512, BLK), F32), i...]
where the time goes in v4:
time: 69.6 us; the launch traced here: 69.5 us
  Pallas kernels  66.5 us (96%)
  local copies, waits for them, and re-layouts  2.37 us (3%)
    pallas_call x1, Pallas kernels, local(): pl.pallas_call(kernel, out_shape=jax.ShapeDtypeStruct((512, BLK), F32), i...  66.5 us
    broadcast_in_dim x1, local copies, waits for them, and re-layouts, local(): return out[:, None, :]  2.37 us

profile of v4, /device:TPU:1, one launch (start us, length us, event | category | flops | bytes accessed | tf_op | source)
XLA Modules:
  0.0 69.5 jit_solution(2799436713735987426)
XLA Ops:
  0.7 66.5 %far_field.1 = f32[512,256]{1,0:T(8,128)} custom-call(f32[512,256]{1,0:T(8,128)} %dens_h.1, f32[1,256]{1,0:T(1,128)} %bitcast.3, f32[3,256]{1,0:T(4,128)} %coords_h.1, s32[1]{0:T(128)S(6)} %copy.7.counts, f32[3,1,8192]{2,1,0:T(1,128)} %wave_h.1), custom_call_target="tpu_custom_call" | custom-call | flops 8600000512 | bytes 2000000 | tf_op jit(solution)/shard_map/far_field/pallas_call | solution.py:380
  67.1 2.4 %copy.6 = f32[512,1,256]{2,1,0:T(1,128)} copy(f32[512,1,256]{2,0,1:T(8,128)} %bitcast.2) | data formatting | bytes 1048576 | tf_op jit(solution)/shard_map/broadcast_in_dim | solution.py:429

commit v5 on v4

--- a/solution.py
+++ b/solution.py
@@ -116,6 +116,36 @@
     for ch in range(NCH):
         W[ch, 0:HB] = ((w * dens[ch * HB : (ch + 1) * HB, :]) * scale).astype(BF16)
         W[ch, HB:] = ((w * dens[256 + ch * HB : 256 + (ch + 1) * HB, :]) * scale).astype(BF16)
+    for d in n1:
+        d.wait_recv()
+    eight = jnp.zeros((8, 128), I32)
+    line = lax.broadcasted_iota(I32, (8, 128), 0)
+    for k in range(8):
+        eight = jnp.where(line == k, cnt1[k], eight)
+    me16 = x * N + y
+    cnt2[me16] = eight
+    n2 = [
+        remote(cnt2.at[me16], cnt2.at[me16], s2s.at[k], s2r.at[k], peers16[k]) for k in range(15)
+    ]
+    for d in n2:
+        d.start()
+
+    raw[own, 0:3] = coords[...]
+    dg = [
+        remote(raw.at[own], raw.at[own], sgs.at[k], sgr.at[k], dev(x, up(y, i), c, up(z, j)))
+        for k, (i, j) in enumerate(peersyz)
+    ]
+    for d in dg:
+        d.start()
+
+    def end_copy(k):
+        return remote(raw.at[own], raw.at[16 + runy], sxs.at[k], sxr.at[runy], group[k])
+
+    @pl.when(z == N - 1)
+    def _():
+        for k in range(16):
+            end_copy(k).start()
+
     kf[...] = jnp.zeros_like(kf)
     for t, dx in enumerate((2, 1, 3, 0)):
         for h in range(2):
@@ -129,36 +159,6 @@
     turns = jnp.concatenate([k1, k2, k1, k3, k2, k1, jnp.zeros((80, NDIR), F32)], 0).astype(BF16)
     for t in range(4):
         kmat[t] = turns[:, t * 512 : (t + 1) * 512]
-
-    for d in n1:
-        d.wait_recv()
-    eight = jnp.zeros((8, 128), I32)
-    line = lax.broadcasted_iota(I32, (8, 128), 0)
-    for k in range(8):
-        eight = jnp.where(line == k, cnt1[k], eight)
-    me16 = x * N + y
-    cnt2[me16] = eight
-    n2 = [
-        remote(cnt2.at[me16], cnt2.at[me16], s2s.at[k], s2r.at[k], peers16[k]) for k in range(15)
-    ]
-    for d in n2:
-        d.start()
-
-    raw[own, 0:3] = coords[...]
-    dg = [
-        remote(raw.at[own], raw.at[own], sgs.at[k], sgr.at[k], dev(x, up(y, i), c, up(z, j)))
-        for k, (i, j) in enumerate(peersyz)
-    ]
-    for d in dg:
-        d.start()
-
-    def end_copy(k):
-        return remote(raw.at[own], raw.at[16 + runy], sxs.at[k], sxr.at[runy], group[k])
-
-    @pl.when(z == N - 1)
-    def _():
-        for k in range(16):
-            end_copy(k).start()
 
     for d in n2:
         d.wait_recv()

time: 69.6 us -> 69.7 us (level)
  no operation moved by 1% of the time
where the time goes in v5:
time: 69.7 us; the launch traced here: 69.4 us
  Pallas kernels  66.4 us (95%)
  local copies, waits for them, and re-layouts  2.37 us (3%)
    pallas_call x1, Pallas kernels, local(): pl.pallas_call(kernel, out_shape=jax.ShapeDtypeStruct((512, BLK), F32), i...  66.4 us
    broadcast_in_dim x1, local copies, waits for them, and re-layouts, local(): return out[:, None, :]  2.37 us

profile of v5, /device:TPU:1, one launch (start us, length us, event | category | flops | bytes accessed | tf_op | source)
XLA Modules:
  0.0 69.4 jit_solution(2383168666737620227)
XLA Ops:
  0.7 66.4 %far_field.1 = f32[512,256]{1,0:T(8,128)} custom-call(f32[512,256]{1,0:T(8,128)} %dens_h.1, f32[1,256]{1,0:T(1,128)} %bitcast.3, f32[3,256]{1,0:T(4,128)} %coords_h.1, s32[1]{0:T(128)S(6)} %copy.7.counts, f32[3,1,8192]{2,1,0:T(1,128)} %wave_h.1), custom_call_target="tpu_custom_call" | custom-call | flops 8600000512 | bytes 2000000 | tf_op jit(solution)/shard_map/far_field/pallas_call | solution.py:380
  67.1 2.4 %copy.6 = f32[512,1,256]{2,1,0:T(1,128)} copy(f32[512,1,256]{2,0,1:T(8,128)} %bitcast.2) | data formatting | bytes 1048576 | tf_op jit(solution)/shard_map/broadcast_in_dim | solution.py:429
